TPU v7x, 32 devices: a whole 2x2x4 slice. The times are simulated.
32 devices in a mesh: outer: 8 (over y, x, core), inner: 4 (over z).
Axes of the slice: x: 2, y: 2, z: 4, core: 2. Of those that a mesh axis runs over, the one named last changes fastest.
Arguments:
- query_proj: bfloat16 [49152, 2048], P(('outer', 'inner')), may hold values from -6 to 6
- key_proj: bfloat16 [49152, 2048], P(('outer', 'inner')), may hold values from -6 to 6
- value_proj: bfloat16 [49152, 2048], P(('outer', 'inner')), may hold values from -6 to 6
- norm_gain: float32 [2048], replicated, may hold values from 0.25 to 1.75
Outputs:
- attended: bfloat16 [49152, 2048], P(('outer', 'inner'))
All inputs are finite; a program needn't handle non-finite values.
Results may differ from a plain program's by a relative error of at most 0.0049.
Values sent between devices are 32-bit elements; how exact they have to be, the bound alone decides.
A program may use at most 192 MiB of HBM per device.

v0:
```python
import jax
import jax.numpy as jnp
from jax import lax
from jax.sharding import PartitionSpec as P

H = 16
DK = 128
SPAN = 256


def prefix_2(array, axis, combine, identity):
    size, place = (lax.axis_size(axis), lax.axis_index(axis))
    everything = lax.all_gather(array, axis)
    start = jnp.broadcast_to(jnp.asarray(identity, array.dtype), array.shape)

    def step(k, before):
        reached = k < place
        new = combine(before, everything[k])
        return jnp.where(reached, new, before)

    return lax.fori_loop(0, size, step, start)


def add_states(earlier, later):
    return earlier + later


def shards(query_proj, key_proj, value_proj, norm_gain):
    tokens = query_proj.shape[0]
    count = tokens // SPAN
    shape = (count, SPAN, H, DK)
    queries = query_proj.reshape(shape)
    keys_local = key_proj.reshape(shape)
    values_local = value_proj.reshape(shape)
    block_states = jnp.einsum(
        "nchd,nche->nhde", keys_local, values_local, preferred_element_type=jnp.float32
    )
    total = jnp.sum(block_states, axis=0)
    flat = total.reshape(1, H * DK * DK)
    shares = lax.all_to_all(flat, "inner", split_axis=1, concat_axis=0, tiled=True)
    share_within = jnp.cumsum(shares, axis=0) - shares
    share_total = jnp.sum(shares, axis=0)
    share_earlier = prefix_2(share_total, "outer", add_states, jnp.zeros_like(share_total))
    share_prefix = share_within + share_earlier[None]
    mine = lax.all_to_all(share_prefix, "inner", split_axis=0, concat_axis=1, tiled=True)
    prefix = mine.reshape(H, DK, DK)
    running = jnp.cumsum(block_states, axis=0) - block_states
    boundary = (prefix[None] + running).astype(jnp.bfloat16)
    carried = jnp.einsum("nchd,nhde->nche", queries, boundary, preferred_element_type=jnp.float32)
    positions = jnp.arange(SPAN)
    causal = positions[:, None] >= positions[None, :]
    scores = jnp.einsum("nchd,nshd->nhcs", queries, keys_local, preferred_element_type=jnp.float32)
    scores = jnp.where(causal[None, None], scores, 0.0).astype(jnp.bfloat16)
    local = jnp.einsum("nhcs,nshe->nche", scores, values_local, preferred_element_type=jnp.float32)
    raw = carried + local
    meansq = jnp.mean(raw * raw, axis=-1, keepdims=True)
    normed = raw * lax.rsqrt(meansq + 1e-06) * norm_gain.reshape(H, DK)
    return normed.astype(jnp.bfloat16).reshape(tokens, H * DK)


def solution(mesh):
    return jax.shard_map(
        shards,
        mesh=mesh,
        in_specs=(
            P(("outer", "inner"), None),
            P(("outer", "inner"), None),
            P(("outer", "inner"), None),
            P(),
        ),
        out_specs=P(("outer", "inner"), None),
        check_vma=False,
    )
```

profile of v0, /device:TPU:0, one launch (start us, length us, event | category | flops | bytes accessed | tf_op | source)
XLA Modules:
  0.0 222.4 jit_solution(1198121099365172502)
XLA Ops:
  6.5 0.0 all-gather.3.cloned.1.call-start
  6.5 7.8 %copy.26 = bf16[192,8,16,128]{3,2,1,0:T(8,128)(2,1)} copy(bf16[192,8,16,128]{3,1,2,0:T(8,128)(2,1)} %bitcast.47) | data formatting | bytes 12582912
  14.4 9.0 %copy.22 = bf16[6,256,16,128]{1,3,2,0:T(8,128)(2,1)} copy(bf16[6,256,16,128]{3,2,1,0:T(8,128)(2,1)} %bitcast.44) | data formatting | bytes 12582912 | tf_op jit(solution)/shard_map/reshape | solution.py:34
  23.4 7.8 %copy.25 = bf16[192,8,16,128]{3,2,1,0:T(8,128)(2,1)} copy(bf16[192,8,16,128]{3,1,2,0:T(8,128)(2,1)} %bitcast.48) | data formatting | bytes 12582912
  31.3 9.7 %fusion.17 = (f32[16,128,128]{2,1,0:T(8,128)S(1)}, f32[6,16,128,128]{3,2,1,0:T(8,128)}) fusion(bf16[6,256,16,128]{1,3,2,0:T(8,128)(2,1)} %copy.22, bf16[6,256,16,128]{3,2,1,0:T(8,128)(2,1)} %bitcast.41), kind=kOutput, calls=%fused_computation.25 | convolution fusion | flops 806617088 | bytes 19922944 | tf_op jit(solution)/shard_map/nchd,nche->nhde/dot_general | solution.py:35
  40.9 31.8 %all_to_all.23 = f32[1,4,65536]{2,0,1:T(1,128)S(1)} all-to-all(f32[1,4,65536]{2,0,1:T(1,128)S(1)} %bitcast.51), channel_id=1, replica_groups=mesh['outer'=8,'inner'=4] {'inner'}, dimensions={1} | all-to-all | bytes 2097152 | tf_op jit(solution)/shard_map/all_to_all | solution.py:40
  72.7 1.9 reduce_sum.28
  74.7 0.0 all-gather.3.cloned.1.call-update
  74.7 27.1 %all-gather.3.cloned.1.call-done = f32[524288]{0:T(1024)} async-done(((f32[65536]{0:T(1024)}), f32[524288]{0:T(1024)}) %all-gather.3.cloned.1.call-update) | async-done | bytes 2097168 | tf_op jit(solution)/shard_map/all_gather | solution.py:13
  101.9 3.3 %reshape.91 = f32[8,65536]{1,0:T(8,128)} reshape(f32[524288]{0:T(1024)} %all-gather.3.cloned.1.call-done) | data formatting | bytes 4194304 | tf_op jit(solution)/shard_map/all_gather | solution.py:13
  105.1 15.0 %while.14 = (s32[]{:T(128)}, f32[65536]{0:T(1024)S(1)}, s32[]{:T(128)}, f32[8,65536]{1,0:T(8,128)}, s32[]{:T(128)}, /*index=5*/s32[]{:T(128)}) while((s32[]{:T(128)}, f32[65536]{0:T(1024)S(1)}, s32[]{:T(128)}, f32[8,65536]{1,0:T(8,128)}, s32[]{:T(128)}, /*index=5*/s32[]{:T(128)}) %tuple.34), condition=%wide.region_4.5_spmd.clone, body=%wide.region_3.4_spmd.clone.sunk | while | flops 196612 | bytes 1310813 | solution.py:21
  105.1 1.8 constant_dynamic-slice_fusion.2
  106.9 0.1 add_select_fusion.2
  107.0 1.8 constant_dynamic-slice_fusion.2
  108.8 0.1 add_select_fusion.2
  108.9 1.8 constant_dynamic-slice_fusion.2
  110.7 0.1 add_select_fusion.2
  110.8 1.8 constant_dynamic-slice_fusion.2
  112.6 0.1 add_select_fusion.2
  112.6 1.8 constant_dynamic-slice_fusion.2
  114.4 0.1 add_select_fusion.2
  114.5 1.8 constant_dynamic-slice_fusion.2
  116.3 0.1 add_select_fusion.2
  116.4 1.8 constant_dynamic-slice_fusion.2
  118.2 0.1 add_select_fusion.2
  118.3 1.8 constant_dynamic-slice_fusion.2
  120.1 0.1 add_select_fusion.2
  120.2 1.8 fusion
  122.0 0.0 slice-start
  122.0 4.7 %all-to-all-start.1 = ((f32[4,1,65536]{2,1,0:T(1,128)}), f32[4,1,65536]{2,1,0:T(1,128)S(1)}, u32[]{:S(2)}, u32[]{:S(2)}) async-start(f32[4,1,65536]{2,1,0:T(1,128)} %fusion), calls=%async_computation.1 | async-start | bytes 2097152 | tf_op jit(solution)/shard_map/all_to_all | solution.py:45
  126.7 0.0 slice-start.1
  126.7 8.0 %copy.27 = bf16[192,8,16,128]{3,2,1,0:T(8,128)(2,1)} copy(bf16[192,8,16,128]{3,1,2,0:T(8,128)(2,1)} %bitcast.49) | data formatting | bytes 12582912
  134.7 0.0 slice-done
  134.7 0.0 slice-done.1
  134.7 3.2 %fusion.22 = f32[6,16,128,128]{3,2,1,0:T(8,128)} fusion(f32[6,16,128,128]{3,2,1,0:T(8,128)S(1)} %bitcast.39), kind=kOutput, calls=%fused_computation.26 | output fusion | flops 7864320 | bytes 12582912 | tf_op jit(solution)/shard_map/jit(cumsum)/reduce_window_sum | solution.py:47
  137.9 14.9 %all-to-all-done.1 = f32[4,1,65536]{2,1,0:T(1,128)S(1)} async-done(((f32[4,1,65536]{2,1,0:T(1,128)}), f32[4,1,65536]{2,1,0:T(1,128)S(1)}, u32[]{:S(2)}, u32[]{:S(2)}) %all-to-all-start.1) | async-done | bytes 1048608 | tf_op jit(solution)/shard_map/all_to_all | solution.py:45
  152.8 13.6 %fusion.12 = f32[6,16,128,256]{3,2,1,0:T(8,128)} fusion(bf16[6,256,16,128]{3,2,1,0:T(8,128)(2,1)} %bitcast.45, f32[6,16,128,128]{3,2,1,0:T(8,128)} %fusion.22, f32[6,16,128,128]{3,2,1,0:T(8,128)} %get-tuple-element.109, f32[16,128,128]{2,1,0:T(8,128)S(1)} %bitcast.50), kind=kOutput, calls=%fused_computation.18 | convolution fusion | flops 810024960 | bytes 32505856 | tf_op jit(solution)/shard_map/nchd,nhde->nche/dot_general | solution.py:49
  166.4 0.0 copy-start
  166.4 19.4 %multiply_reduce_fusion = (f32[6,256,16]{1,2,0:T(8,128)S(1)}, f32[6,16,256,128]{2,3,1,0:T(8,128)}) fusion(f32[6,16,128,256]{3,2,1,0:T(8,128)} %fusion.12, bf16[6,256,16,128]{1,3,2,0:T(8,128)(2,1)} %copy.22, pred[256,256]{1,0:T(8,128)(4,1)S(1)} %iota_compare_fusion, bf16[6,256,16,128]{3,2,1,0:T(8,128)(2,1)} %bitcast.42, bf16[6,256,16,128]{3,2,1,0:T(8,128)(2,1)} %bitcast.46), kind=kOutput, calls=%fused_computation.8 | convolution fusion | flops 3243220992 | bytes 44204032 | tf_op jit(solution)/shard_map/nhcs,nshe->nche/dot_general | solution.py:54
  185.8 0.0 copy-done
  185.8 12.0 %multiply_convert_fusion = bf16[6,256,16,128]{1,3,2,0:T(8,128)(2,1)} fusion(f32[16,128]{1,0:T(8,128)S(1)} %bitcast.52, f32[6,256,16]{1,2,0:T(8,128)S(1)} %add_rsqrt_fusion, f32[6,16,256,128]{2,3,1,0:T(8,128)} %get-tuple-element.111, f32[6,16,128,256]{3,2,1,0:T(8,128)} %fusion.12), kind=kLoop, calls=%fused_computation.7 | loop fusion | flops 12582912 | bytes 31563776 | tf_op jit(solution)/shard_map/convert_element_type | solution.py:58
  197.8 9.1 %copy.23 = bf16[6,256,16,128]{3,2,1,0:T(8,128)(2,1)} copy(bf16[6,256,16,128]{1,3,2,0:T(8,128)(2,1)} %multiply_convert_fusion) | data formatting | bytes 12582912 | tf_op jit(solution)/shard_map/convert_element_type | solution.py:58
  206.9 8.7 %copy.46 = bf16[192,8,16,128]{3,1,2,0:T(8,128)(2,1)} copy(bf16[192,8,16,128]{3,2,1,0:T(8,128)(2,1)} %bitcast.43) | data formatting | bytes 12582912
  (4 shorter events, 0.1 us)
Async XLA Ops:
  6.5 95.3 %all-gather.3.cloned.1.call-start = ((), (), s32[]{:S(2)}) async-start(), calls=%async_computation.2 | async-start | bytes 2359296 | tf_op jit(solution)/shard_map/all_gather | solution.py:13
  122.0 12.8 %slice-start = ((s8[6291456]{0:T(1024)(128)(4,1)}), s8[2097152]{0:T(1024)(128)(4,1)S(1)}, s32[]{:S(2)}) async-start(s8[6291456]{0:T(1024)(128)(4,1)} %bitcast.38), calls=%async_computation.3 | async-start | bytes 4194304
  122.0 30.9 %all-to-all-start.1 = ((f32[4,1,65536]{2,1,0:T(1,128)}), f32[4,1,65536]{2,1,0:T(1,128)S(1)}, u32[]{:S(2)}, u32[]{:S(2)}) async-start(f32[4,1,65536]{2,1,0:T(1,128)} %fusion), calls=%async_computation.1 | async-start | bytes 2097152 | tf_op jit(solution)/shard_map/all_to_all | solution.py:45
  126.7 8.0 %slice-start.1 = ((s8[6291456]{0:T(1024)(128)(4,1)}), s8[4194304]{0:T(1024)(128)(4,1)S(1)}, s32[]{:S(2)}) async-start(s8[6291456]{0:T(1024)(128)(4,1)} %bitcast.38), calls=%async_computation.4 | async-start | bytes 8388608
  166.4 19.4 %copy-start = (f32[2048]{0:T(1024)S(1)}, f32[2048]{0:T(1024)}, u32[]{:S(2)}) copy-start(f32[2048]{0:T(1024)} %param.9) | copy-start | bytes 24580
Sparse Core Ops, SparseCore 0:
  74.8 26.9 all-gather.2
where the time goes:
time: 223 us; the launch traced here: 222 us
  local copies, waits for them, and re-layouts  68 us (30%)
  matrix products  42.6 us (19%)
  waiting for transfers between devices  42.1 us (19%)
  blocking collectives  31.8 us (14%)
  other arithmetic  19.6 us (9%)
  between operations  13.5 us (6%)
  starting transfers between devices  4.73 us (2%)
    unnamed x10, local copies, waits for them, and re-layouts  32.4 us
    all_to_all x1, blocking collectives, shards(): lax.all_to_all(flat, 'inner', split_axis=1, concat_axis=0, tiled=True)  31.8 us
    all_gather x1, waiting for transfers between devices, prefix_2(): everything = lax.all_gather(array, axis)  27.1 us
    dot_general x1, matrix products, shards(): jnp.einsum('nhcs,nshe->nche', scores, values_local, preferred_element_typ...  19.4 us
    all_to_all x1, waiting for transfers between devices, shards(): lax.all_to_all(share_prefix, 'inner', split_axis=0, concat_axis=1, tiled=...  14.9 us
    dynamic_slice x8, local copies, waits for them, and re-layouts, step(): new = combine(before, everything[k])  14.2 us
    dot_general x1, matrix products, shards(): jnp.einsum('nchd,nhde->nche', queries, boundary, preferred_element_type=j...  13.6 us
    convert_element_type x1, other arithmetic, shards(): return normed.astype(jnp.bfloat16).reshape(tokens, H * DK)  12 us
  transfers between devices with their start and end apart: 2, of which 2 were waited for; matrix products, arithmetic and copies ran while one was open for 5% of the time, Pallas kernels for 0%

commit v1 on v0

v1 whole, which is shorter than its diff:
```python
import functools

import jax
import jax.numpy as jnp
from jax import lax
from jax.experimental import pallas as pl
from jax.experimental.pallas import tpu as pltpu
from jax.sharding import PartitionSpec as P

DK = 128
SPAN = 256
HOP = 2
LOCAL = 4
MESH = pl.DeviceIdType.MESH
F32 = jnp.float32
BF16 = jnp.bfloat16


def dot(a, b, ca, cb):
    return lax.dot_general(a, b, (((ca,), (cb,)), ((), ())), preferred_element_type=F32)


def kernel(
    n_outer, n_inner, heads, count, steps,
    q_hbm, k_hbm, v_hbm, g_ref, o_hbm,
    qb, kb, vb, run, loc, fr, br, fs, bs, xs, xr,
    in_sem, out_sem, f_ss, f_rs, b_ss, b_rs, x_ss, x_rs,
):
    o = lax.axis_index("outer")
    z = lax.axis_index("inner")
    last = n_inner - 1

    def fetch(j, src, dst, h):
        return pltpu.make_async_copy(
            src.at[:, pl.ds(pl.multiple_of(h * DK, DK), DK)], dst.at[h], in_sem.at[j, h]
        )

    def store(h):
        return pltpu.make_async_copy(
            qb.at[h], o_hbm.at[:, pl.ds(pl.multiple_of(h * DK, DK), DK)], out_sem.at[h]
        )

    def forward(h):
        return pltpu.make_async_remote_copy(
            src_ref=fs.at[h], dst_ref=fr.at[h], send_sem=f_ss.at[h], recv_sem=f_rs.at[h],
            device_id=(o, lax.rem(z + 1, n_inner)), device_id_type=MESH,
        )

    def backward(h):
        return pltpu.make_async_remote_copy(
            src_ref=bs.at[h], dst_ref=br.at[h], send_sem=b_ss.at[h], recv_sem=b_rs.at[h],
            device_id=(o, lax.rem(z + last, n_inner)), device_id_type=MESH,
        )

    bits = [lax.rem(o // (1 << k), 2) for k in range(steps)]
    partners = [o + (1 - 2 * bits[k]) * (1 << k) for k in range(steps)]

    def across(k, h):
        return pltpu.make_async_remote_copy(
            src_ref=xs.at[k, h], dst_ref=xr.at[k, h], send_sem=x_ss.at[k, h], recv_sem=x_rs.at[k, h],
            device_id=(partners[k], z), device_id_type=MESH,
        )

    def load_states(h, c):
        fetch(1, k_hbm, kb, h).start()
        fetch(2, v_hbm, vb, h).start()
        return c

    def load_queries(h, c):
        fetch(0, q_hbm, qb, h).start()
        return c

    lax.fori_loop(0, heads, load_states, 0)
    lax.fori_loop(0, heads, load_queries, 0)

    barrier = pltpu.get_barrier_semaphore()
    for k in range(steps):
        pl.semaphore_signal(barrier, inc=1, device_id=(partners[k], z), device_id_type=MESH)

    @pl.when(z > 0)
    def _():
        pl.semaphore_signal(barrier, inc=1, device_id=(o, z - 1), device_id_type=MESH)

    @pl.when(z < last)
    def _():
        pl.semaphore_signal(barrier, inc=1, device_id=(o, z + 1), device_id_type=MESH)

    pl.semaphore_wait(barrier, steps + jnp.minimum(z, 1) + jnp.minimum(last - z, 1))

    def at(t, lag, body):
        h = t - lag

        @pl.when((h >= 0) & (h < heads))
        def _():
            body(h)

    def rows(n):
        return pl.ds(n * SPAN, SPAN)

    def states(h):
        fetch(1, k_hbm, kb, h).wait()
        fetch(2, v_hbm, vb, h).wait()
        total = None
        for n in range(count):
            new = dot(kb[h, rows(n), :], vb[h, rows(n), :], 0, 0)
            total = new if total is None else total + new
            run[h, n] = total

    def go_forward(h):
        @pl.when(z == 0)
        def _():
            fr[h] = jnp.zeros((DK, DK), F32)

        @pl.when(z > 0)
        def _():
            forward(h).wait_recv()

        @pl.when(z < last)
        def _():
            fs[h] = fr[h] + run[h, count - 1]
            forward(h).start()

    def go_backward(h):
        @pl.when(z == last)
        def _():
            br[h] = jnp.zeros((DK, DK), F32)

        @pl.when(z < last)
        def _():
            backward(h).wait_recv()

        @pl.when(z > 0)
        def _():
            bs[h] = br[h] + run[h, count - 1]
            backward(h).start()

    def exchange(k, h):
        if k == 0:
            total = fr[h] + run[h, count - 1] + br[h]
        else:
            total = receive(k - 1, h)
        if k < steps - 1:
            xs[k, h] = total
            across(k, h).start()
        elif k == steps - 1:

            @pl.when(bits[k] == 0)
            def _():
                xs[k, h] = total
                across(k, h).start()

    def receive(k, h):
        across(k, h).wait_recv()
        came = xr[k, h]

        @pl.when(bits[k] == 1)
        def _():
            fr[h] = fr[h] + came

        return xs[k, h] + came

    def local(h):
        fetch(0, q_hbm, qb, h).wait()
        causal = lax.broadcasted_iota(jnp.int32, (SPAN, SPAN), 0) >= lax.broadcasted_iota(
            jnp.int32, (SPAN, SPAN), 1
        )
        for n in range(count):
            scores = dot(qb[h, rows(n), :], kb[h, rows(n), :], 1, 1)
            scores = jnp.where(causal, scores, 0.0).astype(BF16)
            loc[h, rows(n), :] = dot(scores, vb[h, rows(n), :], 1, 0)

    def finish(h):
        if steps:

            @pl.when(bits[steps - 1] == 1)
            def _():
                across(steps - 1, h).wait_recv()
                fr[h] = fr[h] + xr[steps - 1, h]

        gain = g_ref[pl.ds(h, 1), :]
        prefix = fr[h]
        for n in range(count):
            carried = prefix if n == 0 else prefix + run[h, n - 1]
            raw = dot(qb[h, rows(n), :], carried.astype(BF16), 1, 0) + loc[h, rows(n), :]
            meansq = jnp.mean(raw * raw, axis=-1, keepdims=True)
            qb[h, rows(n), :] = (raw * lax.rsqrt(meansq + 1e-06) * gain).astype(BF16)
        store(h).start()

    base = HOP * last

    def step(t, c):
        at(t, 0, states)
        at(t, HOP * z, go_forward)
        at(t, HOP * (last - z), go_backward)
        for k in range(steps):
            at(t, base + HOP * k, functools.partial(exchange, k))
        at(t, LOCAL, local)
        at(t, base + HOP * steps, finish)
        return c

    lax.fori_loop(0, heads + base + HOP * steps, step, 0)

    def drain(h, c):
        store(h).wait()

        @pl.when(z < last)
        def _():
            forward(h).wait_send()

        @pl.when(z > 0)
        def _():
            backward(h).wait_send()

        for k in range(steps - 1):
            across(k, h).wait_send()
        if steps:

            @pl.when(bits[steps - 1] == 0)
            def _():
                across(steps - 1, h).wait_send()

        return c

    lax.fori_loop(0, heads, drain, 0)


def solution(mesh):
    n_outer, n_inner = mesh.shape["outer"], mesh.shape["inner"]
    steps = n_outer.bit_length() - 1
    assert n_outer == 1 << steps

    def shards(query, key, value, gain):
        tokens, width = query.shape
        heads, count = width // DK, tokens // SPAN
        dma = pltpu.SemaphoreType.DMA
        some = max(steps, 1)
        state = (heads, DK, DK)
        return pl.pallas_call(
            functools.partial(kernel, n_outer, n_inner, heads, count, steps),
            out_shape=jax.ShapeDtypeStruct((tokens, width), BF16),
            in_specs=[pl.BlockSpec(memory_space=pl.ANY)] * 3
            + [pl.BlockSpec(memory_space=pltpu.VMEM)],
            out_specs=pl.BlockSpec(memory_space=pl.ANY),
            scratch_shapes=[
                pltpu.VMEM((heads, tokens, DK), BF16),
                pltpu.VMEM((heads, tokens, DK), BF16),
                pltpu.VMEM((heads, tokens, DK), BF16),
                pltpu.VMEM((heads, count, DK, DK), F32),
                pltpu.VMEM((heads, tokens, DK), F32),
                pltpu.VMEM(state, F32),
                pltpu.VMEM(state, F32),
                pltpu.VMEM(state, F32),
                pltpu.VMEM(state, F32),
                pltpu.VMEM((some,) + state, F32),
                pltpu.VMEM((some,) + state, F32),
                dma((3, heads)),
                dma((heads,)),
                dma((heads,)),
                dma((heads,)),
                dma((heads,)),
                dma((heads,)),
                dma((some, heads)),
                dma((some, heads)),
            ],
            compiler_params=pltpu.CompilerParams(
                collective_id=0, has_side_effects=True, vmem_limit_bytes=60 * 1024 * 1024
            ),
        )(query, key, value, gain.reshape(heads, DK))

    return jax.shard_map(
        shards,
        mesh=mesh,
        in_specs=(
            P(("outer", "inner"), None),
            P(("outer", "inner"), None),
            P(("outer", "inner"), None),
            P(),
        ),
        out_specs=P(("outer", "inner"), None),
        check_vma=False,
    )
```

time: 223 us -> 60.5 us (0.27)
  local copies, waits for them, and re-layouts: 68 us -> 6.61 us
  Pallas kernels: 0 us -> 53.4 us
  matrix products: 42.6 us -> 0 us
  waiting for transfers between devices: 42.1 us -> 0 us
  blocking collectives: 31.8 us -> 0 us
  other arithmetic: 19.6 us -> 0 us
  between operations: 13.5 us -> 0.01 us
  starting transfers between devices: 4.73 us -> 0 us
    pallas_call x0 -> x1, Pallas kernels: none -> 53.4 us  [shards(): pl.pallas_call(functools.partial(kernel, n_outer, n_inner, heads, count,...]
    dot_general x3 -> x0, matrix products: 42.6 us -> none  [the longest x1 19.4 us: shards(): jnp.einsum('nhcs,nshe->nche', scores, values_local, preferred_element_typ...]
    all_to_all x1 -> x0, blocking collectives: 31.8 us -> none  [shards(): lax.all_to_all(flat, 'inner', split_axis=1, concat_axis=0, tiled=True)]
    all_gather x1 -> x0, waiting for transfers between devices: 27.1 us -> none  [prefix_2(): everything = lax.all_gather(array, axis)]
    unnamed x10 -> x1, local copies, waits for them, and re-layouts: 32.4 us -> 6.61 us
    all_to_all x1 -> x0, waiting for transfers between devices: 14.9 us -> none  [shards(): lax.all_to_all(share_prefix, 'inner', split_axis=0, concat_axis=1, tiled=...]
    dynamic_slice x8 -> x0, local copies, waits for them, and re-layouts: 14.2 us -> none  [step(): new = combine(before, everything[k])]
    convert_element_type x1 -> x0, other arithmetic: 12 us -> none  [shards(): return normed.astype(jnp.bfloat16).reshape(tokens, H * DK)]
  transfers between devices with their start and end apart: 2 -> 0, of which waited for: 2 -> 0; matrix products, arithmetic and copies ran while one was open for 5% -> 0% of each run, Pallas kernels for 0% -> 0%
where the time goes in v1:
time: 60.5 us; the launch traced here: 60 us
  Pallas kernels  53.4 us (88%)
  local copies, waits for them, and re-layouts  6.61 us (11%)
    pallas_call x1, Pallas kernels, shards(): pl.pallas_call(functools.partial(kernel, n_outer, n_inner, heads, count,...  53.4 us
    unnamed x1, local copies, waits for them, and re-layouts  6.61 us

profile of v1, /device:TPU:0, one launch (start us, length us, event | category | flops | bytes accessed | tf_op | source)
XLA Modules:
  0.0 60.0 jit_solution(13287082881005136017)
XLA Ops:
  0.0 53.4 %shard_map.46 = bf16[1536,2048]{1,0:T(8,128)(2,1)} custom-call(bf16[1536,2048]{1,0:T(8,128)(2,1)} %q_hbm.1, bf16[1536,2048]{1,0:T(8,128)(2,1)} %k_hbm.1, bf16[1536,2048]{1,0:T(8,128)(2,1)} %v_hbm.1, f32[16,128]{1,0:T(8,128)} %bitcast.1), custom_call_target="tpu_custom_call" | custom-call | tf_op jit(solution)/shard_map/pallas_call | solution.py:238
  53.4 6.6 %copy.6 = bf16[1536,2048]{1,0:T(8,128)(2,1)} copy(bf16[1536,2048]{1,0:T(8,128)(2,1)} %shard_map.46) | data formatting | bytes 12582912

commit v2 on v1

--- a/solution.py
+++ b/solution.py
@@ -9,7 +9,9 @@
 
 DK = 128
 SPAN = 256
-HOP = 2
+HOP = 3
+NEAR = 2
+FAR = 3
 LOCAL = 4
 MESH = pl.DeviceIdType.MESH
 F32 = jnp.float32
@@ -22,8 +24,8 @@
 
 def kernel(
     n_outer, n_inner, heads, count, steps,
-    q_hbm, k_hbm, v_hbm, g_ref, o_hbm,
-    qb, kb, vb, run, loc, fr, br, fs, bs, xs, xr,
+    q_hbm, k_hbm, v_hbm, g_hbm, o_hbm,
+    g_ref, g_sem, qb, kb, vb, run, loc, fr, br, fs, bs, xs, xr,
     in_sem, out_sem, f_ss, f_rs, b_ss, b_rs, x_ss, x_rs,
 ):
     o = lax.axis_index("outer")
@@ -72,6 +74,8 @@
 
     lax.fori_loop(0, heads, load_states, 0)
     lax.fori_loop(0, heads, load_queries, 0)
+    gains = pltpu.make_async_copy(g_hbm, g_ref, g_sem)
+    gains.start()
 
     barrier = pltpu.get_barrier_semaphore()
     for k in range(steps):
@@ -186,19 +190,21 @@
             qb[h, rows(n), :] = (raw * lax.rsqrt(meansq + 1e-06) * gain).astype(BF16)
         store(h).start()
 
+    gains.wait()
     base = HOP * last
+    lags = [0] + [NEAR + FAR * k for k in range(steps)]
 
     def step(t, c):
         at(t, 0, states)
         at(t, HOP * z, go_forward)
         at(t, HOP * (last - z), go_backward)
         for k in range(steps):
-            at(t, base + HOP * k, functools.partial(exchange, k))
+            at(t, base + lags[k], functools.partial(exchange, k))
         at(t, LOCAL, local)
-        at(t, base + HOP * steps, finish)
-        return c
-
-    lax.fori_loop(0, heads + base + HOP * steps, step, 0)
+        at(t, base + lags[steps], finish)
+        return c
+
+    lax.fori_loop(0, heads + base + lags[steps], step, 0)
 
     def drain(h, c):
         store(h).wait()
@@ -238,10 +244,11 @@
         return pl.pallas_call(
             functools.partial(kernel, n_outer, n_inner, heads, count, steps),
             out_shape=jax.ShapeDtypeStruct((tokens, width), BF16),
-            in_specs=[pl.BlockSpec(memory_space=pl.ANY)] * 3
-            + [pl.BlockSpec(memory_space=pltpu.VMEM)],
+            in_specs=[pl.BlockSpec(memory_space=pl.ANY)] * 4,
             out_specs=pl.BlockSpec(memory_space=pl.ANY),
             scratch_shapes=[
+                pltpu.VMEM((heads, DK), F32),
+                dma,
                 pltpu.VMEM((heads, tokens, DK), BF16),
                 pltpu.VMEM((heads, tokens, DK), BF16),
                 pltpu.VMEM((heads, tokens, DK), BF16),
@@ -263,7 +270,7 @@
                 dma((some, heads)),
             ],
             compiler_params=pltpu.CompilerParams(
-                collective_id=0, has_side_effects=True, vmem_limit_bytes=60 * 1024 * 1024
+                collective_id=0, has_side_effects=True, vmem_limit_bytes=(41 + 2 * some) * 1024 * 1024
             ),
         )(query, key, value, gain.reshape(heads, DK))
 

time: 60.5 us -> 52.3 us (0.86)
  Pallas kernels: 53.4 us -> 48.6 us
  local copies, waits for them, and re-layouts: 6.61 us -> 3.4 us
    pallas_call x1, Pallas kernels: 53.4 us -> 48.6 us  [shards(): pl.pallas_call(functools.partial(kernel, n_outer, n_inner, heads, count,...]
    unnamed x1 -> x3, local copies, waits for them, and re-layouts: 6.61 us -> 3.4 us
where the time goes in v2:
time: 52.3 us; the launch traced here: 52 us
  Pallas kernels  48.6 us (93%)
  local copies, waits for them, and re-layouts  3.4 us (7%)
    pallas_call x1, Pallas kernels, shards(): pl.pallas_call(functools.partial(kernel, n_outer, n_inner, heads, count,...  48.6 us
    unnamed x3, local copies, waits for them, and re-layouts  3.4 us

profile of v2, /device:TPU:0, one launch (start us, length us, event | category | flops | bytes accessed | tf_op | source)
XLA Modules:
  0.0 52.0 jit_solution(16784629785096916554)
XLA Ops:
  0.0 0.0 copy-start
  0.0 0.7 %copy-done = f32[2048]{0:T(1024)S(1)} copy-done((f32[2048]{0:T(1024)S(1)}, f32[2048]{0:T(1024)}, u32[]{:S(2)}) %copy-start) | copy-done | bytes 8216
  0.7 48.6 %shard_map.46 = bf16[1536,2048]{1,0:T(8,128)(2,1)S(1)} custom-call(bf16[1536,2048]{1,0:T(8,128)(2,1)} %q_hbm.1, bf16[1536,2048]{1,0:T(8,128)(2,1)} %k_hbm.1, bf16[1536,2048]{1,0:T(8,128)(2,1)} %v_hbm.1, f32[16,128]{1,0:T(8,128)S(1)} %bitcast.1), custom_call_target="tpu_custom_call" | custom-call | tf_op jit(solution)/shard_map/pallas_call | solution.py:244
  49.3 2.7 %copy.6 = bf16[1536,2048]{1,0:T(8,128)(2,1)} copy(bf16[1536,2048]{1,0:T(8,128)(2,1)S(1)} %shard_map.46) | data formatting | bytes 12582912
Async XLA Ops:
  0.0 0.7 %copy-start = (f32[2048]{0:T(1024)S(1)}, f32[2048]{0:T(1024)}, u32[]{:S(2)}) copy-start(f32[2048]{0:T(1024)} %param.7) | copy-start | bytes 24580

commit v3 on v2

--- a/solution.py
+++ b/solution.py
@@ -25,12 +25,13 @@
 def kernel(
     n_outer, n_inner, heads, count, steps,
     q_hbm, k_hbm, v_hbm, g_hbm, o_hbm,
-    g_ref, g_sem, qb, kb, vb, run, loc, fr, br, fs, bs, xs, xr,
+    g_ref, g_sem, ex, qb, kb, vb, run, loc, fr, br, fs, bs, xs, xr,
     in_sem, out_sem, f_ss, f_rs, b_ss, b_rs, x_ss, x_rs,
 ):
     o = lax.axis_index("outer")
     z = lax.axis_index("inner")
     last = n_inner - 1
+    half = heads // 2
 
     def fetch(j, src, dst, h):
         return pltpu.make_async_copy(
@@ -64,15 +65,16 @@
         )
 
     def load_states(h, c):
-        fetch(1, k_hbm, kb, h).start()
-        fetch(2, v_hbm, vb, h).start()
+        for g in (h, h + half):
+            fetch(1, k_hbm, kb, g).start()
+            fetch(2, v_hbm, vb, g).start()
         return c
 
     def load_queries(h, c):
         fetch(0, q_hbm, qb, h).start()
         return c
 
-    lax.fori_loop(0, heads, load_states, 0)
+    lax.fori_loop(0, half, load_states, 0)
     lax.fori_loop(0, heads, load_queries, 0)
     gains = pltpu.make_async_copy(g_hbm, g_ref, g_sem)
     gains.start()
@@ -91,12 +93,12 @@
 
     pl.semaphore_wait(barrier, steps + jnp.minimum(z, 1) + jnp.minimum(last - z, 1))
 
-    def at(t, lag, body):
+    def at(t, lag, body, first=0, number=half):
         h = t - lag
 
-        @pl.when((h >= 0) & (h < heads))
-        def _():
-            body(h)
+        @pl.when((h >= 0) & (h < number))
+        def _():
+            body(h + first)
 
     def rows(n):
         return pl.ds(n * SPAN, SPAN)
@@ -110,7 +112,7 @@
             total = new if total is None else total + new
             run[h, n] = total
 
-    def go_forward(h):
+    def go_forward(early, h):
         @pl.when(z == 0)
         def _():
             fr[h] = jnp.zeros((DK, DK), F32)
@@ -121,10 +123,11 @@
 
         @pl.when(z < last)
         def _():
-            fs[h] = fr[h] + run[h, count - 1]
+            mine = run[h, count - 1]
+            fs[h] = fr[h] + (mine if early else mine + ex[h - half])
             forward(h).start()
 
-    def go_backward(h):
+    def go_backward(early, h):
         @pl.when(z == last)
         def _():
             br[h] = jnp.zeros((DK, DK), F32)
@@ -135,33 +138,53 @@
 
         @pl.when(z > 0)
         def _():
-            bs[h] = br[h] + run[h, count - 1]
+            bs[h] = br[h] + (run[h, count - 1] if early else ex[h - half])
             backward(h).start()
 
-    def exchange(k, h):
-        if k == 0:
+    def exchange(early, k, h):
+        if k > 0:
+            total = receive(early, k - 1, h)
+        elif early:
             total = fr[h] + run[h, count - 1] + br[h]
         else:
-            total = receive(k - 1, h)
+            total = run[h, count - 1]
+            ex[h - half] = jnp.zeros((DK, DK), F32)
         if k < steps - 1:
             xs[k, h] = total
             across(k, h).start()
-        elif k == steps - 1:
+        else:
 
             @pl.when(bits[k] == 0)
             def _():
                 xs[k, h] = total
                 across(k, h).start()
 
-    def receive(k, h):
+    def add(early, h, came):
+        if early:
+            fr[h] = fr[h] + came
+        else:
+            ex[h - half] = ex[h - half] + came
+
+    def receive(early, k, h):
         across(k, h).wait_recv()
         came = xr[k, h]
 
         @pl.when(bits[k] == 1)
         def _():
-            fr[h] = fr[h] + came
+            add(early, h, came)
 
         return xs[k, h] + came
+
+    def settle(early, h):
+        if steps == 0:
+            if not early:
+                ex[h - half] = jnp.zeros((DK, DK), F32)
+            return
+
+        @pl.when(bits[steps - 1] == 1)
+        def _():
+            across(steps - 1, h).wait_recv()
+            add(early, h, xr[steps - 1, h])
 
     def local(h):
         fetch(0, q_hbm, qb, h).wait()
@@ -173,14 +196,11 @@
             scores = jnp.where(causal, scores, 0.0).astype(BF16)
             loc[h, rows(n), :] = dot(scores, vb[h, rows(n), :], 1, 0)
 
-    def finish(h):
-        if steps:
-
-            @pl.when(bits[steps - 1] == 1)
-            def _():
-                across(steps - 1, h).wait_recv()
-                fr[h] = fr[h] + xr[steps - 1, h]
-
+    def finish(early, h):
+        if early:
+            settle(early, h)
+        else:
+            fr[h] = fr[h] + ex[h - half] + br[h]
         gain = g_ref[pl.ds(h, 1), :]
         prefix = fr[h]
         for n in range(count):
@@ -194,17 +214,26 @@
     base = HOP * last
     lags = [0] + [NEAR + FAR * k for k in range(steps)]
 
+    bind = functools.partial
+
     def step(t, c):
         at(t, 0, states)
-        at(t, HOP * z, go_forward)
-        at(t, HOP * (last - z), go_backward)
+        at(t, 0, states, half)
+        at(t, HOP * z, bind(go_forward, True))
+        at(t, HOP * (last - z), bind(go_backward, True))
         for k in range(steps):
-            at(t, base + lags[k], functools.partial(exchange, k))
-        at(t, LOCAL, local)
-        at(t, base + lags[steps], finish)
+            at(t, lags[k], bind(exchange, False, k), half)
+        at(t, lags[steps], bind(settle, False), half)
+        at(t, lags[steps] + HOP * z, bind(go_forward, False), half)
+        at(t, lags[steps] + HOP * (last - z), bind(go_backward, False), half)
+        for k in range(steps):
+            at(t, base + lags[k], bind(exchange, True, k))
+        at(t, LOCAL, local, 0, heads)
+        at(t, base + lags[steps], bind(finish, True))
+        at(t, base + lags[steps], bind(finish, False), half)
         return c
 
-    lax.fori_loop(0, heads + base + lags[steps], step, 0)
+    lax.fori_loop(0, half + max(base + lags[steps], half + LOCAL), step, 0)
 
     def drain(h, c):
         store(h).wait()
@@ -249,6 +278,7 @@
             scratch_shapes=[
                 pltpu.VMEM((heads, DK), F32),
                 dma,
+                pltpu.VMEM((heads // 2, DK, DK), F32),
                 pltpu.VMEM((heads, tokens, DK), BF16),
                 pltpu.VMEM((heads, tokens, DK), BF16),
                 pltpu.VMEM((heads, tokens, DK), BF16),
@@ -270,7 +300,7 @@
                 dma((some, heads)),
             ],
             compiler_params=pltpu.CompilerParams(
-                collective_id=0, has_side_effects=True, vmem_limit_bytes=(41 + 2 * some) * 1024 * 1024
+                collective_id=0, has_side_effects=True, vmem_limit_bytes=(38 + 3 * some) * 1024 * 1024
             ),
         )(query, key, value, gain.reshape(heads, DK))
 

time: 52.3 us -> 46.5 us (0.89)
  Pallas kernels: 48.6 us -> 42.9 us
    pallas_call x1, Pallas kernels: 48.6 us -> 42.9 us  [shards(): pl.pallas_call(functools.partial(kernel, n_outer, n_inner, heads, count,...]
where the time goes in v3:
time: 46.5 us; the launch traced here: 46.3 us
  Pallas kernels  42.9 us (92%)
  local copies, waits for them, and re-layouts  3.4 us (7%)
    pallas_call x1, Pallas kernels, shards(): pl.pallas_call(functools.partial(kernel, n_outer, n_inner, heads, count,...  42.9 us
    unnamed x3, local copies, waits for them, and re-layouts  3.4 us

profile of v3, /device:TPU:0, one launch (start us, length us, event | category | flops | bytes accessed | tf_op | source)
XLA Modules:
  0.0 46.3 jit_solution(7956742141375906047)
XLA Ops:
  0.0 0.0 copy-start
  0.0 0.7 %copy-done = f32[2048]{0:T(1024)S(1)} copy-done((f32[2048]{0:T(1024)S(1)}, f32[2048]{0:T(1024)}, u32[]{:S(2)}) %copy-start) | copy-done | bytes 8216
  0.7 42.9 %shard_map.46 = bf16[1536,2048]{1,0:T(8,128)(2,1)S(1)} custom-call(bf16[1536,2048]{1,0:T(8,128)(2,1)} %q_hbm.1, bf16[1536,2048]{1,0:T(8,128)(2,1)} %k_hbm.1, bf16[1536,2048]{1,0:T(8,128)(2,1)} %v_hbm.1, f32[16,128]{1,0:T(8,128)S(1)} %bitcast.1), custom_call_target="tpu_custom_call" | custom-call | tf_op jit(solution)/shard_map/pallas_call | solution.py:273
  43.6 2.7 %copy.6 = bf16[1536,2048]{1,0:T(8,128)(2,1)} copy(bf16[1536,2048]{1,0:T(8,128)(2,1)S(1)} %shard_map.46) | data formatting | bytes 12582912
Async XLA Ops:
  0.0 0.7 %copy-start = (f32[2048]{0:T(1024)S(1)}, f32[2048]{0:T(1024)}, u32[]{:S(2)}) copy-start(f32[2048]{0:T(1024)} %param.7) | copy-start | bytes 24580
